TPU v7x, 32 devices: a whole 2x2x4 slice. The times are simulated.
32 devices in a mesh: grp: 2 (over x), gy: 16 (over z, y, core).
Axes of the slice: x: 2, y: 2, z: 4, core: 2. Of those that a mesh axis runs over, the one named last changes fastest.
Arguments:
- initial: float32 [64, 32, 256], P('gy', 'grp'), parts along dimension 1, may hold values from -1.2 to 1.2
Outputs:
- slab_ends: float32 [4, 64, 32, 256], P(None, 'gy', 'grp'), parts along dimension 2
There are 2 independent parts, one for each index of `grp`. A program takes and returns all parts, laid end to end along the dimension named above; each array names one. Nothing has to cross between parts.
All inputs are finite; a program needn't handle non-finite values.
Results may differ from a plain program's by a relative error of at most 0.00002.
Values sent between devices are 32-bit elements; how exact they have to be, the bound alone decides.
A program may use at most 128 MiB of HBM per device.

v0:
```python
from functools import partial

import jax
import jax.numpy as jnp
from jax import lax
from jax.sharding import PartitionSpec as P

SLABS = 4


left_weights = (5.0 / 24.0, 1.0 / 3.0, -1.0 / 24.0)
right_weights = (-1.0 / 24.0, 1.0 / 3.0, 5.0 / 24.0)
slab_time = 0.25
half_step = 0.125
fine_coefficient = 1.0
coarse_coefficient = 0.25


def padded_2(block, sides, width):
    for axis, dim in sides:
        count = lax.axis_size(axis)
        forward = [(i, i + 1) for i in range(count - 1)]
        forward.append((count - 1, 0))
        backward = [(target, source) for source, target in forward]
        low = lax.ppermute(
            lax.slice_in_dim(block, block.shape[dim] - width, None, axis=dim), axis, forward
        )
        high = lax.ppermute(lax.slice_in_dim(block, 0, width, axis=dim), axis, backward)
        block = jnp.concatenate([low, block, high], axis=dim)
    return block


def padded_tendency(padded, coefficient):
    center = padded[..., 1:-1, :, :]
    beside = padded[..., 2:, :, :] + padded[..., :-2, :, :]
    beside = beside + jnp.roll(center, 1, -2) + jnp.roll(center, -1, -2)
    beside = beside + jnp.roll(center, 1, -1) + jnp.roll(center, -1, -1)
    return coefficient * (beside - 6.0 * center) + (center - center * center * center)


def quadrature(weights_row, first_term, middle_term, last_term):
    return slab_time * (
        weights_row[0] * first_term + weights_row[1] * middle_term + weights_row[2] * last_term
    )


def advance(node_value, new_tendency, old_tendency, forcing):
    return node_value + (half_step * (new_tendency - old_tendency) + forcing)


def restrict(field):
    sizes_now = field.shape
    blocks = field.reshape(
        sizes_now[:-3] + (sizes_now[-3] // 2, 2, sizes_now[-2] // 2, 2, sizes_now[-1] // 2, 2)
    )
    return jnp.mean(blocks, axis=(-5, -3, -1))


def alternate(even_rows, odd_rows, along):
    paired = jnp.stack([even_rows, odd_rows], axis=along)
    new_shape = list(even_rows.shape)
    new_shape[along] = 2 * new_shape[along]
    return paired.reshape(new_shape)


def stretch(coarse, along):
    even_rows = 0.75 * coarse + 0.25 * jnp.roll(coarse, 1, along)
    odd_rows = 0.75 * coarse + 0.25 * jnp.roll(coarse, -1, along)
    return alternate(even_rows, odd_rows, along)


def prolong_padded(padded):
    center = padded[..., 1:-1, :, :]
    even_rows = 0.75 * center + 0.25 * padded[..., :-2, :, :]
    odd_rows = 0.75 * center + 0.25 * padded[..., 2:, :, :]
    fine_rows = alternate(even_rows, odd_rows, -3)
    return stretch(stretch(fine_rows, -2), -1)


def spread_terms(start_tendency):
    rest_zero = quadrature(left_weights, start_tendency, start_tendency, start_tendency)
    rest_one = quadrature(right_weights, start_tendency, start_tendency, start_tendency)
    return (start_tendency, rest_zero, start_tendency, rest_one)


def stored_terms(forcing_slab, start_tendency):
    return (forcing_slab[0], forcing_slab[1], forcing_slab[2], forcing_slab[3])


def build_forcing(coarse_tendency, mismatch):
    rest_zero = quadrature(
        left_weights, coarse_tendency[:, 0], coarse_tendency[:, 1], coarse_tendency[:, 2]
    ) + quadrature(left_weights, mismatch[:, 0], mismatch[:, 1], mismatch[:, 2])
    rest_one = quadrature(
        right_weights, coarse_tendency[:, 0], coarse_tendency[:, 1], coarse_tendency[:, 2]
    ) + quadrature(right_weights, mismatch[:, 0], mismatch[:, 1], mismatch[:, 2])
    return jnp.stack([coarse_tendency[:, 0], rest_zero, coarse_tendency[:, 1], rest_one], 1)


def coarse_slab(start_value, slab_terms):
    start_padded = padded_2(start_value, (("gy", 0),), 1)
    start_tendency = padded_tendency(start_padded, coarse_coefficient)
    fold_zero, rest_zero, fold_one, rest_one = slab_terms(start_tendency)
    node_one = advance(start_value, start_tendency, fold_zero, rest_zero)
    middle_padded = padded_2(node_one, (("gy", 0),), 1)
    node_two = advance(
        node_one, padded_tendency(middle_padded, coarse_coefficient), fold_one, rest_one
    )
    return (node_one, node_two)


def body(initial):
    first_coarse = restrict(initial)
    node_list = []
    start_value = first_coarse
    for slab_index in range(SLABS):
        node_one, node_two = coarse_slab(start_value, spread_terms)
        node_list.append(jnp.stack([start_value, node_one, node_two]))
        start_value = node_two
    rimmed_coarse = padded_2(jnp.stack(node_list), (("gy", 2),), 1)
    old_iterate = prolong_padded(rimmed_coarse).at[0, 0].set(initial)
    widened = padded_2(old_iterate, (("gy", 2),), 1)
    old_tendency = padded_tendency(widened, fine_coefficient)
    tend_zero = old_tendency[:, 0]
    tend_one = old_tendency[:, 1]
    tend_two = old_tendency[:, 2]
    new_one = advance(
        old_iterate[:, 0],
        tend_zero,
        tend_zero,
        quadrature(left_weights, tend_zero, tend_one, tend_two),
    )
    padded_one = padded_2(new_one, (("gy", 1),), 1)
    new_tend_one = padded_tendency(padded_one, fine_coefficient)
    new_two = advance(
        new_one, new_tend_one, tend_one, quadrature(right_weights, tend_zero, tend_one, tend_two)
    )
    padded_two = padded_2(new_two, (("gy", 1),), 1)
    new_tend_two = padded_tendency(padded_two, fine_coefficient)
    coarse_old = restrict(jnp.stack([old_iterate[:, 0], new_one, new_two], 1))
    padded_old = padded_2(coarse_old, (("gy", 2),), 1)
    coarse_tendency = padded_tendency(padded_old, coarse_coefficient)
    fine_average = restrict(jnp.stack([tend_zero, new_tend_one, new_tend_two], 1))
    forcing = build_forcing(coarse_tendency, fine_average - coarse_tendency)
    difference_list = []
    start_value = first_coarse
    for slab_index in range(SLABS):
        node_one, node_two = coarse_slab(start_value, partial(stored_terms, forcing[slab_index]))
        difference_list.append(node_two - coarse_old[slab_index, 2])
        start_value = node_two
    padded_difference = padded_2(jnp.stack(difference_list), (("gy", 1),), 1)
    return new_two + prolong_padded(padded_difference)


def solution(mesh):
    in_specs = (P("gy", "grp", None),)
    out_specs = P(None, "gy", "grp", None)
    return jax.shard_map(body, mesh=mesh, in_specs=in_specs, out_specs=out_specs, check_vma=False)
```

profile of v0, /device:TPU:0, one launch (start us, length us, event | category | flops | bytes accessed | tf_op | source)
XLA Modules:
  0.0 274.2 jit_solution(6490353799836159689)
XLA Ops:
  0.0 6.3 %reshape.449 = f32[2,2,8,2,128,2]{5,4,3,2,1,0:T(8,128)} reshape(f32[4,16,256]{2,1,0:T(8,128)} %param.3) | data formatting | bytes 131072 | tf_op jit(solution)/shard_map/reshape | solution.py:53
  6.3 2.5 reduce_sum.27
  8.9 5.5 %collective-permute-start = (f32[1,8,128]{2,1,0:T(8,128)S(1)}, f32[1,8,128]{2,1,0:T(8,128)S(1)}, u32[]{:S(2)}, u32[]{:S(2)}) collective-permute-start(f32[1,8,128]{2,1,0:T(8,128)S(1)} %get-tuple-element.266), channel_id=1, source_target_pairs={{1,0},{2,1},{3,2},{4,3},{5,4},{6,5},{7,6},{8,7},{9,8},{10,9},{11,1... | collective-permute-start | bytes 12296 | tf_op jit(solution)/shard_map/ppermute | solution.py:28
  14.5 1.2 collective-permute-done
  15.7 4.4 %collective-permute-done.1 = f32[1,8,128]{2,1,0:T(8,128)S(1)} collective-permute-done((f32[1,8,128]{2,1,0:T(8,128)S(1)}, f32[1,8,128]{2,1,0:T(8,128)S(1)}, u32[]{:S(2)}, u32[]{:S(2)}) %collective-permute-start.1) | collective-permute-done | bytes 4128 | tf_op jit(solution)/shard_map/ppermute | solution.py:25
  21.7 4.4 %collective-permute-done.3 = f32[1,8,128]{2,1,0:T(8,128)S(1)} collective-permute-done((f32[1,8,128]{2,1,0:T(8,128)S(1)}, f32[1,8,128]{2,1,0:T(8,128)S(1)}, u32[]{:S(2)}, u32[]{:S(2)}) %collective-permute-start.3) | collective-permute-done | bytes 4128 | tf_op jit(solution)/shard_map/ppermute | solution.py:25
  27.7 4.4 %collective-permute-done.5 = f32[1,8,128]{2,1,0:T(8,128)S(1)} collective-permute-done((f32[1,8,128]{2,1,0:T(8,128)S(1)}, f32[1,8,128]{2,1,0:T(8,128)S(1)}, u32[]{:S(2)}, u32[]{:S(2)}) %collective-permute-start.5) | collective-permute-done | bytes 4128 | tf_op jit(solution)/shard_map/ppermute | solution.py:25
  33.7 4.5 %collective-permute-done.7 = f32[1,8,128]{2,1,0:T(8,128)S(1)} collective-permute-done((f32[1,8,128]{2,1,0:T(8,128)S(1)}, f32[1,8,128]{2,1,0:T(8,128)S(1)}, u32[]{:S(2)}, u32[]{:S(2)}) %collective-permute-start.7) | collective-permute-done | bytes 4128 | tf_op jit(solution)/shard_map/ppermute | solution.py:25
  39.8 4.4 %collective-permute-done.9 = f32[1,8,128]{2,1,0:T(8,128)S(1)} collective-permute-done((f32[1,8,128]{2,1,0:T(8,128)S(1)}, f32[1,8,128]{2,1,0:T(8,128)S(1)}, u32[]{:S(2)}, u32[]{:S(2)}) %collective-permute-start.9) | collective-permute-done | bytes 4128 | tf_op jit(solution)/shard_map/ppermute | solution.py:25
  45.8 4.5 %collective-permute-done.11 = f32[1,8,128]{2,1,0:T(8,128)S(1)} collective-permute-done((f32[1,8,128]{2,1,0:T(8,128)S(1)}, f32[1,8,128]{2,1,0:T(8,128)S(1)}, u32[]{:S(2)}, u32[]{:S(2)}) %collective-permute-start.11) | collective-permute-done | bytes 4128 | tf_op jit(solution)/shard_map/ppermute | solution.py:25
  51.8 4.4 %collective-permute-done.13 = f32[1,8,128]{2,1,0:T(8,128)S(1)} collective-permute-done((f32[1,8,128]{2,1,0:T(8,128)S(1)}, f32[1,8,128]{2,1,0:T(8,128)S(1)}, u32[]{:S(2)}, u32[]{:S(2)}) %collective-permute-start.13) | collective-permute-done | bytes 4128 | tf_op jit(solution)/shard_map/ppermute | solution.py:25
  57.8 4.5 %collective-permute-done.15 = f32[1,8,128]{2,1,0:T(8,128)S(1)} collective-permute-done((f32[1,8,128]{2,1,0:T(8,128)S(1)}, f32[1,8,128]{2,1,0:T(8,128)S(1)}, u32[]{:S(2)}, u32[]{:S(2)}) %collective-permute-start.15) | collective-permute-done | bytes 4128 | tf_op jit(solution)/shard_map/ppermute | solution.py:25
  62.5 4.4 %collective-permute-start.17 = (f32[4,3,1,8,128]{4,3,2,1,0:T(8,128)S(1)}, f32[4,3,1,8,128]{4,3,2,1,0:T(8,128)S(1)}, u32[]{:S(2)}, u32[]{:S(2)}) collective-permute-start(f32[4,3,1,8,128]{4,3,2,1,0:T(8,128)S(1)} %get-tuple-element.108), channel_id=1, source_target_pairs={{1,0},{2,1},{3,2},{4,3},{5,4},{6,5},{7,6},{8,7},{9,8},{10,9},{11,1... | collective-permute-start | bytes 147464 | tf_op jit(solution)/shard_map/ppermute | solution.py:28
  66.9 1.8 collective-permute-done.16
  70.5 6.4 %copy.377 = f32[4,3,4,16,128,2]{3,5,4,2,1,0:T(2,128)} copy(f32[4,3,4,16,128,2]{4,3,2,1,0,5:T(8,128)S(1)} %pad_maximum_fusion.2) | data formatting | bytes 1572864 | tf_op jit(solution)/shard_map/stack | solution.py:60
  76.8 4.3 %copy.378 = f32[4,3,4,16,256]{4,3,2,0,1:T(8,128)S(1)} copy(f32[4,3,4,16,256]{3,4,2,1,0:T(8,128)} %bitcast.267) | data formatting | bytes 1572864 | tf_op jit(solution)/shard_map/reshape | solution.py:63
  82.2 4.5 %collective-permute-start.18 = (f32[4,3,1,16,256]{4,3,2,1,0:T(8,128)S(1)}, f32[4,3,1,16,256]{4,3,2,1,0:T(8,128)S(1)}, u32[]{:S(2)}, u32[]{:S(2)}) collective-permute-start(f32[4,3,1,16,256]{4,3,2,1,0:T(8,128)S(1)} %copy.379), channel_id=1, source_target_pairs={{1,0},{2,1},{3,2},{4,3},{5,4},{6,5},{7,6},{8,7},{9,8},{10,9},{11,1... | collective-permute-start | bytes 589832 | tf_op jit(solution)/shard_map/ppermute | solution.py:28
  87.4 2.8 %collective-permute-done.19 = f32[4,3,1,16,256]{4,3,2,1,0:T(8,128)S(1)} collective-permute-done((f32[4,3,1,16,256]{4,3,2,1,0:T(8,128)S(1)}, f32[4,3,1,16,256]{4,3,2,1,0:T(8,128)S(1)}, u32[]{:S(2)}, u32[]{:S(2)}) %collective-permute-start.19) | collective-permute-done | bytes 196640 | tf_op jit(solution)/shard_map/ppermute | solution.py:25
  91.4 4.4 %collective-permute-start.20 = (f32[4,1,16,256]{3,2,1,0:T(8,128)S(1)}, f32[4,1,16,256]{3,2,1,0:T(8,128)S(1)}, u32[]{:S(2)}, u32[]{:S(2)}) collective-permute-start(f32[4,1,16,256]{3,2,1,0:T(8,128)S(1)} %get-tuple-element.67), channel_id=1, source_target_pairs={{1,0},{2,1},{3,2},{4,3},{5,4},{6,5},{7,6},{8,7},{9,8},{10,9},{11,1... | collective-permute-start | bytes 196616 | tf_op jit(solution)/shard_map/ppermute | solution.py:28
  95.9 4.7 %copy.398 = f32[4,1,4,16,256]{0,4,3,2,1:T(8,128)} copy(f32[4,1,4,16,256]{4,3,2,0,1:T(8,128)S(1)} %slice_bitcast_fusion.4) | data formatting | bytes 524288 | tf_op jit(solution)/shard_map/slice | solution.py:124
  100.6 4.7 %copy.393 = f32[4,1,4,16,256]{0,4,3,2,1:T(8,128)} copy(f32[4,1,4,16,256]{4,3,2,0,1:T(8,128)S(1)} %get-tuple-element.35) | data formatting | bytes 524288 | tf_op jit(solution)/shard_map/slice | solution.py:128
  105.3 4.7 %copy.394 = f32[4,1,4,16,256]{0,4,3,2,1:T(8,128)} copy(f32[4,1,4,16,256]{4,3,2,0,1:T(8,128)S(1)} %get-tuple-element.36) | data formatting | bytes 524288 | tf_op jit(solution)/shard_map/add | solution.py:48
  110.0 1.0 fusion.25
  112.5 0.8 fusion.256
  113.3 0.9 fusion.254
  114.2 4.7 %copy.395 = f32[4,4,16,256]{0,3,2,1:T(8,128)} copy(f32[4,4,16,256]{3,2,1,0:T(8,128)S(1)} %get-tuple-element.25) | data formatting | bytes 524288 | tf_op jit(solution)/shard_map/add | solution.py:48
  118.9 35.3 %maximum_reduce_fusion = f32[4,3,2,8,128]{0,4,3,2,1:T(8,128)S(1)} fusion(f32[4,1,2,2,8,2,128,2]{0,7,6,5,4,3,2,1:T(2,128)} %bitcast.266, f32[4,1,2,2,8,2,128,2]{0,7,6,5,4,3,2,1:T(2,128)} %bitcast.263, f32[4,1,2,2,8,2,128,2]{0,7,6,5,4,3,2,1:T(2,128)} %bitcast.262), kind=kLoop, calls=%fused_computation | loop fusion | flops 565248 | bytes 884736 | tf_op jit(solution)/shard_map/reduce_sum | solution.py:56
  154.2 1.8 copy.396
  156.0 1.0 broadcast_multiply_fusion.4
  159.8 4.4 %collective-permute-start.24 = (f32[4,1,16,256]{3,2,1,0:T(8,128)}, f32[4,1,16,256]{3,2,1,0:T(8,128)S(1)}, u32[]{:S(2)}, u32[]{:S(2)}) collective-permute-start(f32[4,1,16,256]{3,2,1,0:T(8,128)} %get-tuple-element.65), channel_id=1, source_target_pairs={{1,0},{2,1},{3,2},{4,3},{5,4},{6,5},{7,6},{8,7},{9,8},{10,9},{11,1... | collective-permute-start | bytes 196616 | tf_op jit(solution)/shard_map/ppermute | solution.py:28
  164.8 5.7 %copy.399 = f32[4,4,16,256]{0,3,2,1:T(8,128)} copy(f32[4,4,16,256]{3,2,1,0:T(8,128)} %get-tuple-element.26) | data formatting | bytes 524288 | tf_op jit(solution)/shard_map/add | solution.py:38
  170.6 4.4 %collective-permute-start.22 = (f32[4,3,1,8,128]{4,3,2,1,0:T(8,128)}, f32[4,3,1,8,128]{4,3,2,1,0:T(8,128)}, u32[]{:S(2)}, u32[]{:S(2)}) collective-permute-start(f32[4,3,1,8,128]{4,3,2,1,0:T(8,128)} %get-tuple-element.95), channel_id=1, source_target_pairs={{1,0},{2,1},{3,2},{4,3},{5,4},{6,5},{7,6},{8,7},{9,8},{10,9},{11,1... | collective-permute-start | bytes 147464 | tf_op jit(solution)/shard_map/ppermute | solution.py:28
  175.3 4.7 %copy.400 = f32[4,4,16,256]{0,3,2,1:T(8,128)} copy(f32[4,4,16,256]{3,2,1,0:T(8,128)S(1)} %fusion.10) | data formatting | bytes 524288 | tf_op jit(solution)/shard_map/add | solution.py:38
  180.0 35.3 %maximum_reduce_fusion.1 = f32[4,3,2,8,128]{0,4,3,2,1:T(8,128)S(1)} fusion(f32[4,1,2,2,8,2,128,2]{0,7,6,5,4,3,2,1:T(2,128)} %bitcast.265, f32[4,1,2,2,8,2,128,2]{0,7,6,5,4,3,2,1:T(2,128)} %bitcast.264, f32[4,1,2,2,8,2,128,2]{0,7,6,5,4,3,2,1:T(2,128)} %bitcast.261), kind=kLoop, calls=%fused_computation.1 | loop fusion | flops 565248 | bytes 884736 | tf_op jit(solution)/shard_map/reduce_sum | solution.py:56
  215.3 1.8 copy.401
  217.1 1.4 multiply_subtract_fusion.4
  218.7 4.4 %collective-permute-start.26 = (f32[1,8,128]{2,1,0:T(8,128)S(1)}, f32[1,8,128]{2,1,0:T(8,128)S(1)}, u32[]{:S(2)}, u32[]{:S(2)}) collective-permute-start(f32[1,8,128]{2,1,0:T(8,128)S(1)} %get-tuple-element.181), channel_id=1, source_target_pairs={{1,0},{2,1},{3,2},{4,3},{5,4},{6,5},{7,6},{8,7},{9,8},{10,9},{11,1... | collective-permute-start | bytes 12296 | tf_op jit(solution)/shard_map/ppermute | solution.py:28
  223.2 1.3 collective-permute-done.26
  224.5 4.4 %collective-permute-done.27 = f32[1,8,128]{2,1,0:T(8,128)S(1)} collective-permute-done((f32[1,8,128]{2,1,0:T(8,128)S(1)}, f32[1,8,128]{2,1,0:T(8,128)S(1)}, u32[]{:S(2)}, u32[]{:S(2)}) %collective-permute-start.27) | collective-permute-done | bytes 4128 | tf_op jit(solution)/shard_map/ppermute | solution.py:25
  230.5 4.4 %collective-permute-done.29 = f32[1,8,128]{2,1,0:T(8,128)S(1)} collective-permute-done((f32[1,8,128]{2,1,0:T(8,128)S(1)}, f32[1,8,128]{2,1,0:T(8,128)S(1)}, u32[]{:S(2)}, u32[]{:S(2)}) %collective-permute-start.29) | collective-permute-done | bytes 4128 | tf_op jit(solution)/shard_map/ppermute | solution.py:25
  236.5 4.4 %collective-permute-done.31 = f32[1,8,128]{2,1,0:T(8,128)S(1)} collective-permute-done((f32[1,8,128]{2,1,0:T(8,128)S(1)}, f32[1,8,128]{2,1,0:T(8,128)S(1)}, u32[]{:S(2)}, u32[]{:S(2)}) %collective-permute-start.31) | collective-permute-done | bytes 4128 | tf_op jit(solution)/shard_map/ppermute | solution.py:25
  242.5 4.4 %collective-permute-done.33 = f32[1,8,128]{2,1,0:T(8,128)S(1)} collective-permute-done((f32[1,8,128]{2,1,0:T(8,128)S(1)}, f32[1,8,128]{2,1,0:T(8,128)S(1)}, u32[]{:S(2)}, u32[]{:S(2)}) %collective-permute-start.33) | collective-permute-done | bytes 4128 | tf_op jit(solution)/shard_map/ppermute | solution.py:25
  248.5 4.4 %collective-permute-done.35 = f32[1,8,128]{2,1,0:T(8,128)S(1)} collective-permute-done((f32[1,8,128]{2,1,0:T(8,128)S(1)}, f32[1,8,128]{2,1,0:T(8,128)S(1)}, u32[]{:S(2)}, u32[]{:S(2)}) %collective-permute-start.35) | collective-permute-done | bytes 4128 | tf_op jit(solution)/shard_map/ppermute | solution.py:25
  254.5 4.4 %collective-permute-done.37 = f32[1,8,128]{2,1,0:T(8,128)S(1)} collective-permute-done((f32[1,8,128]{2,1,0:T(8,128)S(1)}, f32[1,8,128]{2,1,0:T(8,128)S(1)}, u32[]{:S(2)}, u32[]{:S(2)}) %collective-permute-start.37) | collective-permute-done | bytes 4128 | tf_op jit(solution)/shard_map/ppermute | solution.py:25
  260.5 4.5 %collective-permute-done.39 = f32[1,8,128]{2,1,0:T(8,128)S(1)} collective-permute-done((f32[1,8,128]{2,1,0:T(8,128)S(1)}, f32[1,8,128]{2,1,0:T(8,128)S(1)}, u32[]{:S(2)}, u32[]{:S(2)}) %collective-permute-start.39) | collective-permute-done | bytes 4128 | tf_op jit(solution)/shard_map/ppermute | solution.py:25
  265.2 4.4 %collective-permute-start.41 = (f32[4,1,8,128]{3,2,1,0:T(8,128)S(1)}, f32[4,1,8,128]{3,2,1,0:T(8,128)S(1)}, u32[]{:S(2)}, u32[]{:S(2)}) collective-permute-start(f32[4,1,8,128]{3,2,1,0:T(8,128)S(1)} %get-tuple-element.120), channel_id=1, source_target_pairs={{1,0},{2,1},{3,2},{4,3},{5,4},{6,5},{7,6},{8,7},{9,8},{10,9},{11,1... | collective-permute-start | bytes 49160 | tf_op jit(solution)/shard_map/ppermute | solution.py:28
  269.6 1.4 collective-permute-done.40
  271.8 1.1 copy.412
  (231 shorter events, 32.8 us)
Async XLA Ops:
  8.9 6.8 %collective-permute-start = (f32[1,8,128]{2,1,0:T(8,128)S(1)}, f32[1,8,128]{2,1,0:T(8,128)S(1)}, u32[]{:S(2)}, u32[]{:S(2)}) collective-permute-start(f32[1,8,128]{2,1,0:T(8,128)S(1)} %get-tuple-element.266), channel_id=1, source_target_pairs={{1,0},{2,1},{3,2},{4,3},{5,4},{6,5},{7,6},{8,7},{9,8},{10,9},{11,1... | collective-permute-start | bytes 12296 | tf_op jit(solution)/shard_map/ppermute | solution.py:28
  14.4 5.7 %collective-permute-start.1 = (f32[1,8,128]{2,1,0:T(8,128)S(1)}, f32[1,8,128]{2,1,0:T(8,128)S(1)}, u32[]{:S(2)}, u32[]{:S(2)}) collective-permute-start(f32[1,8,128]{2,1,0:T(8,128)S(1)} %get-tuple-element.267), channel_id=1, source_target_pairs={{0,1},{1,2},{2,3},{3,4},{4,5},{5,6},{6,7},{7,8},{8,9},{9,10},{10,1... | collective-permute-start | bytes 12296 | tf_op jit(solution)/shard_map/ppermute | solution.py:25
  20.4 1.3 collective-permute-start.2
  20.4 5.8 %collective-permute-start.3 = (f32[1,8,128]{2,1,0:T(8,128)S(1)}, f32[1,8,128]{2,1,0:T(8,128)S(1)}, u32[]{:S(2)}, u32[]{:S(2)}) collective-permute-start(f32[1,8,128]{2,1,0:T(8,128)S(1)} %get-tuple-element.265), channel_id=1, source_target_pairs={{0,1},{1,2},{2,3},{3,4},{4,5},{5,6},{6,7},{7,8},{8,9},{9,10},{10,1... | collective-permute-start | bytes 12296 | tf_op jit(solution)/shard_map/ppermute | solution.py:25
  26.4 1.3 collective-permute-start.4
  26.4 5.8 %collective-permute-start.5 = (f32[1,8,128]{2,1,0:T(8,128)S(1)}, f32[1,8,128]{2,1,0:T(8,128)S(1)}, u32[]{:S(2)}, u32[]{:S(2)}) collective-permute-start(f32[1,8,128]{2,1,0:T(8,128)S(1)} %get-tuple-element.247), channel_id=1, source_target_pairs={{0,1},{1,2},{2,3},{3,4},{4,5},{5,6},{6,7},{7,8},{8,9},{9,10},{10,1... | collective-permute-start | bytes 12296 | tf_op jit(solution)/shard_map/ppermute | solution.py:25
  32.4 1.3 collective-permute-start.6
  32.4 5.8 %collective-permute-start.7 = (f32[1,8,128]{2,1,0:T(8,128)S(1)}, f32[1,8,128]{2,1,0:T(8,128)S(1)}, u32[]{:S(2)}, u32[]{:S(2)}) collective-permute-start(f32[1,8,128]{2,1,0:T(8,128)S(1)} %get-tuple-element.245), channel_id=1, source_target_pairs={{0,1},{1,2},{2,3},{3,4},{4,5},{5,6},{6,7},{7,8},{8,9},{9,10},{10,1... | collective-permute-start | bytes 12296 | tf_op jit(solution)/shard_map/ppermute | solution.py:25
  38.4 1.3 collective-permute-start.8
  38.4 5.8 %collective-permute-start.9 = (f32[1,8,128]{2,1,0:T(8,128)S(1)}, f32[1,8,128]{2,1,0:T(8,128)S(1)}, u32[]{:S(2)}, u32[]{:S(2)}) collective-permute-start(f32[1,8,128]{2,1,0:T(8,128)S(1)} %get-tuple-element.227), channel_id=1, source_target_pairs={{0,1},{1,2},{2,3},{3,4},{4,5},{5,6},{6,7},{7,8},{8,9},{9,10},{10,1... | collective-permute-start | bytes 12296 | tf_op jit(solution)/shard_map/ppermute | solution.py:25
  44.5 1.3 collective-permute-start.10
  44.5 5.8 %collective-permute-start.11 = (f32[1,8,128]{2,1,0:T(8,128)S(1)}, f32[1,8,128]{2,1,0:T(8,128)S(1)}, u32[]{:S(2)}, u32[]{:S(2)}) collective-permute-start(f32[1,8,128]{2,1,0:T(8,128)S(1)} %get-tuple-element.225), channel_id=1, source_target_pairs={{0,1},{1,2},{2,3},{3,4},{4,5},{5,6},{6,7},{7,8},{8,9},{9,10},{10,1... | collective-permute-start | bytes 12296 | tf_op jit(solution)/shard_map/ppermute | solution.py:25
  50.5 1.3 collective-permute-start.12
  50.5 5.8 %collective-permute-start.13 = (f32[1,8,128]{2,1,0:T(8,128)S(1)}, f32[1,8,128]{2,1,0:T(8,128)S(1)}, u32[]{:S(2)}, u32[]{:S(2)}) collective-permute-start(f32[1,8,128]{2,1,0:T(8,128)S(1)} %get-tuple-element.207), channel_id=1, source_target_pairs={{0,1},{1,2},{2,3},{3,4},{4,5},{5,6},{6,7},{7,8},{8,9},{9,10},{10,1... | collective-permute-start | bytes 12296 | tf_op jit(solution)/shard_map/ppermute | solution.py:25
  56.5 1.3 collective-permute-start.14
  56.5 5.8 %collective-permute-start.15 = (f32[1,8,128]{2,1,0:T(8,128)S(1)}, f32[1,8,128]{2,1,0:T(8,128)S(1)}, u32[]{:S(2)}, u32[]{:S(2)}) collective-permute-start(f32[1,8,128]{2,1,0:T(8,128)S(1)} %get-tuple-element.205), channel_id=1, source_target_pairs={{0,1},{1,2},{2,3},{3,4},{4,5},{5,6},{6,7},{7,8},{8,9},{9,10},{10,1... | collective-permute-start | bytes 12296 | tf_op jit(solution)/shard_map/ppermute | solution.py:25
  62.4 6.3 %collective-permute-start.16 = (f32[4,3,1,8,128]{4,3,2,1,0:T(8,128)S(1)}, f32[4,3,1,8,128]{4,3,2,1,0:T(8,128)S(1)}, u32[]{:S(2)}, u32[]{:S(2)}) collective-permute-start(f32[4,3,1,8,128]{4,3,2,1,0:T(8,128)S(1)} %get-tuple-element.107), channel_id=1, source_target_pairs={{0,1},{1,2},{2,3},{3,4},{4,5},{5,6},{6,7},{7,8},{8,9},{9,10},{10,1... | collective-permute-start | bytes 147464 | tf_op jit(solution)/shard_map/ppermute | solution.py:25
  62.5 6.2 %collective-permute-start.17 = (f32[4,3,1,8,128]{4,3,2,1,0:T(8,128)S(1)}, f32[4,3,1,8,128]{4,3,2,1,0:T(8,128)S(1)}, u32[]{:S(2)}, u32[]{:S(2)}) collective-permute-start(f32[4,3,1,8,128]{4,3,2,1,0:T(8,128)S(1)} %get-tuple-element.108), channel_id=1, source_target_pairs={{1,0},{2,1},{3,2},{4,3},{5,4},{6,5},{7,6},{8,7},{9,8},{10,9},{11,1... | collective-permute-start | bytes 147464 | tf_op jit(solution)/shard_map/ppermute | solution.py:28
  82.2 8.0 %collective-permute-start.19 = (f32[4,3,1,16,256]{4,3,2,1,0:T(8,128)S(1)}, f32[4,3,1,16,256]{4,3,2,1,0:T(8,128)S(1)}, u32[]{:S(2)}, u32[]{:S(2)}) collective-permute-start(f32[4,3,1,16,256]{4,3,2,1,0:T(8,128)S(1)} %copy.381), channel_id=1, source_target_pairs={{0,1},{1,2},{2,3},{3,4},{4,5},{5,6},{6,7},{7,8},{8,9},{9,10},{10,1... | collective-permute-start | bytes 589832 | tf_op jit(solution)/shard_map/ppermute | solution.py:25
  82.2 7.9 %collective-permute-start.18 = (f32[4,3,1,16,256]{4,3,2,1,0:T(8,128)S(1)}, f32[4,3,1,16,256]{4,3,2,1,0:T(8,128)S(1)}, u32[]{:S(2)}, u32[]{:S(2)}) collective-permute-start(f32[4,3,1,16,256]{4,3,2,1,0:T(8,128)S(1)} %copy.379), channel_id=1, source_target_pairs={{1,0},{2,1},{3,2},{4,3},{5,4},{6,5},{7,6},{8,7},{9,8},{10,9},{11,1... | collective-permute-start | bytes 589832 | tf_op jit(solution)/shard_map/ppermute | solution.py:28
  91.4 18.6 %collective-permute-start.20 = (f32[4,1,16,256]{3,2,1,0:T(8,128)S(1)}, f32[4,1,16,256]{3,2,1,0:T(8,128)S(1)}, u32[]{:S(2)}, u32[]{:S(2)}) collective-permute-start(f32[4,1,16,256]{3,2,1,0:T(8,128)S(1)} %get-tuple-element.67), channel_id=1, source_target_pairs={{1,0},{2,1},{3,2},{4,3},{5,4},{6,5},{7,6},{8,7},{9,8},{10,9},{11,1... | collective-permute-start | bytes 196616 | tf_op jit(solution)/shard_map/ppermute | solution.py:28
  95.9 14.1 %collective-permute-start.21 = (f32[4,1,16,256]{3,2,1,0:T(8,128)S(1)}, f32[4,1,16,256]{3,2,1,0:T(8,128)S(1)}, u32[]{:S(2)}, u32[]{:S(2)}) collective-permute-start(f32[4,1,16,256]{3,2,1,0:T(8,128)S(1)} %get-tuple-element.68), channel_id=1, source_target_pairs={{0,1},{1,2},{2,3},{3,4},{4,5},{5,6},{6,7},{7,8},{8,9},{9,10},{10,1... | collective-permute-start | bytes 196616 | tf_op jit(solution)/shard_map/ppermute | solution.py:25
  156.0 19.1 %copy-start.2 = (f32[4,4,16,255]{3,2,1,0:T(8,128)S(1)}, f32[4,4,16,255]{3,2,1,0:T(8,128)}, u32[]{:S(2)}) copy-start(f32[4,4,16,255]{3,2,1,0:T(8,128)} %get-tuple-element.57) | copy-start | bytes 783364
  156.0 19.1 %copy-start.3 = (f32[4,4,16,255]{3,2,1,0:T(8,128)S(1)}, f32[4,4,16,255]{3,2,1,0:T(8,128)}, u32[]{:S(2)}) copy-start(f32[4,4,16,255]{3,2,1,0:T(8,128)} %get-tuple-element.58) | copy-start | bytes 783364
  156.0 19.1 %copy-start.4 = (f32[4,4,16,1]{3,2,1,0:T(8,128)S(1)}, f32[4,4,16,1]{3,2,1,0:T(8,128)}, u32[]{:S(2)}) copy-start(f32[4,4,16,1]{3,2,1,0:T(8,128)} %get-tuple-element.59) | copy-start | bytes 3076
  156.0 19.1 %copy-start.5 = (f32[4,4,16,1]{3,2,1,0:T(8,128)S(1)}, f32[4,4,16,1]{3,2,1,0:T(8,128)}, u32[]{:S(2)}) copy-start(f32[4,4,16,1]{3,2,1,0:T(8,128)} %get-tuple-element.60) | copy-start | bytes 3076
  159.8 15.3 %collective-permute-start.24 = (f32[4,1,16,256]{3,2,1,0:T(8,128)}, f32[4,1,16,256]{3,2,1,0:T(8,128)S(1)}, u32[]{:S(2)}, u32[]{:S(2)}) collective-permute-start(f32[4,1,16,256]{3,2,1,0:T(8,128)} %get-tuple-element.65), channel_id=1, source_target_pairs={{1,0},{2,1},{3,2},{4,3},{5,4},{6,5},{7,6},{8,7},{9,8},{10,9},{11,1... | collective-permute-start | bytes 196616 | tf_op jit(solution)/shard_map/ppermute | solution.py:28
  164.2 10.8 %collective-permute-start.25 = (f32[4,1,16,256]{3,2,1,0:T(8,128)}, f32[4,1,16,256]{3,2,1,0:T(8,128)S(1)}, u32[]{:S(2)}, u32[]{:S(2)}) collective-permute-start(f32[4,1,16,256]{3,2,1,0:T(8,128)} %get-tuple-element.66), channel_id=1, source_target_pairs={{0,1},{1,2},{2,3},{3,4},{4,5},{5,6},{6,7},{7,8},{8,9},{9,10},{10,1... | collective-permute-start | bytes 196616 | tf_op jit(solution)/shard_map/ppermute | solution.py:25
  170.6 46.5 %collective-permute-start.22 = (f32[4,3,1,8,128]{4,3,2,1,0:T(8,128)}, f32[4,3,1,8,128]{4,3,2,1,0:T(8,128)}, u32[]{:S(2)}, u32[]{:S(2)}) collective-permute-start(f32[4,3,1,8,128]{4,3,2,1,0:T(8,128)} %get-tuple-element.95), channel_id=1, source_target_pairs={{1,0},{2,1},{3,2},{4,3},{5,4},{6,5},{7,6},{8,7},{9,8},{10,9},{11,1... | collective-permute-start | bytes 147464 | tf_op jit(solution)/shard_map/ppermute | solution.py:28
  175.0 42.1 %collective-permute-start.23 = (f32[4,3,1,8,128]{4,3,2,1,0:T(8,128)}, f32[4,3,1,8,128]{4,3,2,1,0:T(8,128)}, u32[]{:S(2)}, u32[]{:S(2)}) collective-permute-start(f32[4,3,1,8,128]{4,3,2,1,0:T(8,128)} %get-tuple-element.96), channel_id=1, source_target_pairs={{0,1},{1,2},{2,3},{3,4},{4,5},{5,6},{6,7},{7,8},{8,9},{9,10},{10,1... | collective-permute-start | bytes 147464 | tf_op jit(solution)/shard_map/ppermute | solution.py:25
  180.0 37.1 %copy-start.7 = (f32[4,3,2,1,128]{4,3,2,1,0:T(1,128)S(1)}, f32[4,3,2,1,128]{4,3,2,1,0:T(1,128)}, u32[]{:S(2)}) copy-start(f32[4,3,2,1,128]{4,3,2,1,0:T(1,128)} %get-tuple-element.97) | copy-start | bytes 36868
  180.0 37.1 %copy-start.8 = (f32[4,3,2,1,128]{4,3,2,1,0:T(1,128)S(1)}, f32[4,3,2,1,128]{4,3,2,1,0:T(1,128)}, u32[]{:S(2)}) copy-start(f32[4,3,2,1,128]{4,3,2,1,0:T(1,128)} %get-tuple-element.98) | copy-start | bytes 36868
  218.7 5.8 %collective-permute-start.26 = (f32[1,8,128]{2,1,0:T(8,128)S(1)}, f32[1,8,128]{2,1,0:T(8,128)S(1)}, u32[]{:S(2)}, u32[]{:S(2)}) collective-permute-start(f32[1,8,128]{2,1,0:T(8,128)S(1)} %get-tuple-element.181), channel_id=1, source_target_pairs={{1,0},{2,1},{3,2},{4,3},{5,4},{6,5},{7,6},{8,7},{9,8},{10,9},{11,1... | collective-permute-start | bytes 12296 | tf_op jit(solution)/shard_map/ppermute | solution.py:28
  223.1 5.7 %collective-permute-start.27 = (f32[1,8,128]{2,1,0:T(8,128)S(1)}, f32[1,8,128]{2,1,0:T(8,128)S(1)}, u32[]{:S(2)}, u32[]{:S(2)}) collective-permute-start(f32[1,8,128]{2,1,0:T(8,128)S(1)} %get-tuple-element.182), channel_id=1, source_target_pairs={{0,1},{1,2},{2,3},{3,4},{4,5},{5,6},{6,7},{7,8},{8,9},{9,10},{10,1... | collective-permute-start | bytes 12296 | tf_op jit(solution)/shard_map/ppermute | solution.py:25
  229.1 1.3 collective-permute-start.28
  229.1 5.8 %collective-permute-start.29 = (f32[1,8,128]{2,1,0:T(8,128)S(1)}, f32[1,8,128]{2,1,0:T(8,128)S(1)}, u32[]{:S(2)}, u32[]{:S(2)}) collective-permute-start(f32[1,8,128]{2,1,0:T(8,128)S(1)} %get-tuple-element.180), channel_id=1, source_target_pairs={{0,1},{1,2},{2,3},{3,4},{4,5},{5,6},{6,7},{7,8},{8,9},{9,10},{10,1... | collective-permute-start | bytes 12296 | tf_op jit(solution)/shard_map/ppermute | solution.py:25
  235.1 1.3 collective-permute-start.30
  235.1 5.8 %collective-permute-start.31 = (f32[1,8,128]{2,1,0:T(8,128)S(1)}, f32[1,8,128]{2,1,0:T(8,128)S(1)}, u32[]{:S(2)}, u32[]{:S(2)}) collective-permute-start(f32[1,8,128]{2,1,0:T(8,128)S(1)} %get-tuple-element.162), channel_id=1, source_target_pairs={{0,1},{1,2},{2,3},{3,4},{4,5},{5,6},{6,7},{7,8},{8,9},{9,10},{10,1... | collective-permute-start | bytes 12296 | tf_op jit(solution)/shard_map/ppermute | solution.py:25
  241.2 1.3 collective-permute-start.32
  241.2 5.8 %collective-permute-start.33 = (f32[1,8,128]{2,1,0:T(8,128)S(1)}, f32[1,8,128]{2,1,0:T(8,128)S(1)}, u32[]{:S(2)}, u32[]{:S(2)}) collective-permute-start(f32[1,8,128]{2,1,0:T(8,128)S(1)} %get-tuple-element.160), channel_id=1, source_target_pairs={{0,1},{1,2},{2,3},{3,4},{4,5},{5,6},{6,7},{7,8},{8,9},{9,10},{10,1... | collective-permute-start | bytes 12296 | tf_op jit(solution)/shard_map/ppermute | solution.py:25
  247.2 1.3 collective-permute-start.34
  247.2 5.8 %collective-permute-start.35 = (f32[1,8,128]{2,1,0:T(8,128)S(1)}, f32[1,8,128]{2,1,0:T(8,128)S(1)}, u32[]{:S(2)}, u32[]{:S(2)}) collective-permute-start(f32[1,8,128]{2,1,0:T(8,128)S(1)} %get-tuple-element.142), channel_id=1, source_target_pairs={{0,1},{1,2},{2,3},{3,4},{4,5},{5,6},{6,7},{7,8},{8,9},{9,10},{10,1... | collective-permute-start | bytes 12296 | tf_op jit(solution)/shard_map/ppermute | solution.py:25
  253.2 1.3 collective-permute-start.36
  253.2 5.8 %collective-permute-start.37 = (f32[1,8,128]{2,1,0:T(8,128)S(1)}, f32[1,8,128]{2,1,0:T(8,128)S(1)}, u32[]{:S(2)}, u32[]{:S(2)}) collective-permute-start(f32[1,8,128]{2,1,0:T(8,128)S(1)} %get-tuple-element.140), channel_id=1, source_target_pairs={{0,1},{1,2},{2,3},{3,4},{4,5},{5,6},{6,7},{7,8},{8,9},{9,10},{10,1... | collective-permute-start | bytes 12296 | tf_op jit(solution)/shard_map/ppermute | solution.py:25
  259.2 1.3 collective-permute-start.38
  259.2 5.8 %collective-permute-start.39 = (f32[1,8,128]{2,1,0:T(8,128)S(1)}, f32[1,8,128]{2,1,0:T(8,128)S(1)}, u32[]{:S(2)}, u32[]{:S(2)}) collective-permute-start(f32[1,8,128]{2,1,0:T(8,128)S(1)} %get-tuple-element.130), channel_id=1, source_target_pairs={{0,1},{1,2},{2,3},{3,4},{4,5},{5,6},{6,7},{7,8},{8,9},{9,10},{10,1... | collective-permute-start | bytes 12296 | tf_op jit(solution)/shard_map/ppermute | solution.py:25
  265.1 5.9 %collective-permute-start.40 = (f32[4,1,8,128]{3,2,1,0:T(8,128)S(1)}, f32[4,1,8,128]{3,2,1,0:T(8,128)S(1)}, u32[]{:S(2)}, u32[]{:S(2)}) collective-permute-start(f32[4,1,8,128]{3,2,1,0:T(8,128)S(1)} %get-tuple-element.119), channel_id=1, source_target_pairs={{0,1},{1,2},{2,3},{3,4},{4,5},{5,6},{6,7},{7,8},{8,9},{9,10},{10,1... | collective-permute-start | bytes 49160 | tf_op jit(solution)/shard_map/ppermute | solution.py:25
  265.2 5.9 %collective-permute-start.41 = (f32[4,1,8,128]{3,2,1,0:T(8,128)S(1)}, f32[4,1,8,128]{3,2,1,0:T(8,128)S(1)}, u32[]{:S(2)}, u32[]{:S(2)}) collective-permute-start(f32[4,1,8,128]{3,2,1,0:T(8,128)S(1)} %get-tuple-element.120), channel_id=1, source_target_pairs={{1,0},{2,1},{3,2},{4,3},{5,4},{6,5},{7,6},{8,7},{9,8},{10,9},{11,1... | collective-permute-start | bytes 49160 | tf_op jit(solution)/shard_map/ppermute | solution.py:28
  (3 other events, 49.0 us)
where the time goes:
time: 275 us; the launch traced here: 274 us
  waiting for transfers between devices  85.6 us (31%)
  other arithmetic  81.4 us (30%)
  local copies, waits for them, and re-layouts  63.1 us (23%)
  starting transfers between devices  43.5 us (16%)
    reduce_sum x3, other arithmetic, restrict(): return jnp.mean(blocks, axis=(-5, -3, -1))  73.1 us
    ppermute x21, waiting for transfers between devices, padded_2(): lax.ppermute(lax.slice_in_dim(block, block.shape[dim] - width, None, axis...  72.4 us
    ppermute x21, starting transfers between devices, padded_2(): lax.ppermute(lax.slice_in_dim(block, 0, width, axis=dim), axis, backward)  36.7 us
    ppermute x21, waiting for transfers between devices, padded_2(): lax.ppermute(lax.slice_in_dim(block, 0, width, axis=dim), axis, backward)  13.2 us
    add x2, local copies, waits for them, and re-layouts, padded_tendency(): coefficient * (beside - 6.0 * center) + (center - center * center * center)  10.5 us
    add x2, local copies, waits for them, and re-layouts, advance(): return node_value + (half_step * (new_tendency - old_tendency) + forcing)  9.4 us
    another operation x6, local copies, waits for them, and re-layouts, alternate(): paired = jnp.stack([even_rows, odd_rows], axis=along)  7.92 us
    ppermute x21, starting transfers between devices, padded_2(): lax.ppermute(lax.slice_in_dim(block, block.shape[dim] - width, None, axis...  6.81 us
  transfers between devices with their start and end apart: 42, of which 33 were waited for; matrix products, arithmetic and copies ran while one was open for 23% of the time, Pallas kernels for 0%

commit v1 on v0

v1 whole, which is shorter than its diff:
```python
import jax
import jax.numpy as jnp
from jax import lax
from jax.experimental import pallas as pl
from jax.experimental.pallas import tpu as pltpu
from jax.sharding import PartitionSpec as P

SLABS = 4
slab_time = 0.25
half_step = 0.125
left_weights = (5.0 / 24.0, 1.0 / 3.0, -1.0 / 24.0)
right_weights = (-1.0 / 24.0, 1.0 / 3.0, 5.0 / 24.0)
Q0 = tuple(slab_time * w for w in left_weights)
Q1 = tuple(slab_time * w for w in right_weights)

REACH = 5
OWN = 2
PARITIES = ((0, 0), (0, 1), (1, 0), (1, 1))


def lanes(x, shift):
    return pltpu.roll(x, shift % x.shape[-1], x.ndim - 1)


def rows(x, shift):
    return pltpu.roll(x, shift % x.shape[-2], x.ndim - 2)


def coarse_step(v):
    c = v[1:-1]
    beside = (v[2:] + v[:-2]) + (rows(c, 1) + rows(c, -1)) + (lanes(c, 1) + lanes(c, -1))
    return 0.03125 * beside + c * (0.9375 - 0.125 * (c * c))


def coarse_tendency(v):
    c = v[1:-1]
    beside = (v[2:] + v[:-2]) + (rows(c, 1) + rows(c, -1)) + (lanes(c, 1) + lanes(c, -1))
    return 0.25 * beside - c * (0.5 + c * c)


def fine_tendency(v):
    c = [p[1:-1] for p in v]
    out = []
    for k, (px, pz) in enumerate(PARITIES):
        x = c[2 * (1 - px) + pz]
        z = c[2 * px + 1 - pz]
        beside = (v[k][2:] + v[k][:-2]) + (x + rows(x, -1 if px else 1)) + (z + lanes(z, -1 if pz else 1))
        out.append(beside - c[k] * (5.0 + c[k] * c[k]))
    return out


def prolong(c):
    c = c * (1.0 / 64.0)
    triple = 3.0 * c
    out = []
    by_z = (triple + lanes(c, 1), triple + lanes(c, -1))
    planes = {}
    for pz in (0, 1):
        w = by_z[pz]
        triple = 3.0 * w
        planes[0, pz] = triple + rows(w, 1)
        planes[1, pz] = triple + rows(w, -1)
    for k in PARITIES:
        p = planes[k]
        triple = 3.0 * p
        odd = triple[:-1] + p[1:]
        even = triple[1:] + p[:-1]
        out.append(jnp.stack([odd, even], 1).reshape((2 * odd.shape[0],) + odd.shape[1:]))
    return out


def restrict(v):
    s = (v[0] + v[1]) + (v[2] + v[3])
    s = s.reshape((s.shape[0] // 2, 2) + s.shape[1:])
    return 0.125 * (s[:, 0] + s[:, 1])


def pick(x, table):
    high = x.astype(jnp.bfloat16)
    rest = x - high.astype(jnp.float32)
    middle = rest.astype(jnp.bfloat16)
    low = (rest - middle.astype(jnp.float32)).astype(jnp.bfloat16)
    dot = lambda p: jnp.dot(p, table, preferred_element_type=jnp.float32)
    return (dot(high) + dot(middle)) + dot(low)


def kernel(count, init_ref, out_ref, raw, fine, coarse, force0, force1, force2, force3, ends, new, stage, obuf,
           in_sem, out_sem, send_sem, recv_sem):
    me = lax.axis_index("gy")
    force = (force0, force1, force2, force3)

    def device(offset):
        return {"gy": lax.rem(me + (offset + count), count)}

    fetch = pltpu.make_async_copy(init_ref, raw, in_sem)
    fetch.start()
    barrier = pltpu.get_barrier_semaphore()
    for d in range(1, REACH + 1):
        for offset in (d, -d):
            pl.semaphore_signal(barrier, inc=1, device_id=device(offset))

    copies = []

    def send(src, dst, offset):
        k = len(copies)
        copy = pltpu.make_async_remote_copy(
            src_ref=src, dst_ref=dst, send_sem=send_sem.at[k], recv_sem=recv_sem.at[k], device_id=device(offset))
        copy.start()
        copies.append(copy)
        return copy

    a = lax.broadcasted_iota(jnp.int32, (256, 256), 0)
    b = lax.broadcasted_iota(jnp.int32, (256, 256), 1)
    part = (a == 2 * lax.rem(b, 128) + lax.div(b, 128)).astype(jnp.float32).astype(jnp.bfloat16)
    join = (b == 2 * lax.rem(a, 128) + lax.div(a, 128)).astype(jnp.float32).astype(jnp.bfloat16)

    fetch.wait()
    y = pick(raw[...].reshape(64, 256), part)
    stage[0, 0] = y[:, :128]
    stage[0, 1] = y[:, 128:]
    own = [stage[0, pz, pl.ds(px, 32, 2)].reshape(4, 8, 128) for px, pz in PARITIES]
    coarse[pl.ds(2 * REACH, OWN)] = restrict(own)
    for k in range(4):
        fine[pl.ds(3, 4), k] = own[k]

    pl.semaphore_wait(barrier, 2 * REACH)
    first_sends = []
    for d in range(REACH, 0, -1):
        for offset in (d, -d):
            first_sends.append(send(coarse.at[pl.ds(2 * REACH, OWN)],
                                    coarse.at[pl.ds(2 * REACH - 2 * offset, OWN)], offset))
    fine_sends = [send(fine.at[pl.ds(4, 3)], fine.at[pl.ds(0, 3)], 1),
                  send(fine.at[pl.ds(3, 3)], fine.at[pl.ds(7, 3)], -1)]

    for copy in first_sends:
        copy.wait_recv()
    s = coarse[...]
    nodes = [s[8:14]]
    for k in range(1, 9):
        s = coarse_step(s)
        nodes.append(s[8 - k:14 - k])

    for copy in fine_sends:
        copy.wait_recv()
    force_sends = []
    for n in range(SLABS):
        if n == 0:
            old0 = [fine[:, k] for k in range(4)]
        else:
            old0 = prolong(nodes[2 * n])
        old1 = prolong(nodes[2 * n + 1])
        old2 = prolong(nodes[2 * n + 2])
        f0 = fine_tendency(old0)
        f1 = fine_tendency(old1)
        f2 = fine_tendency(old2)
        one = [o[1:-1] + ((Q0[0] * x + Q0[1] * y) + Q0[2] * z) for o, x, y, z in zip(old0, f0, f1, f2)]
        g1 = fine_tendency(one)
        two = [o[1:-1] + (half_step * g + ((Q1[0] * x[1:-1] + (Q1[1] - half_step) * y[1:-1]) + Q1[2] * z[1:-1]))
               for o, g, x, y, z in zip(one, g1, f0, f1, f2)]
        g2 = fine_tendency(two)
        for k in range(4):
            new[n, k] = two[k][1:5]
        ends[pl.ds(1, 2), n] = restrict([t[1:5] for t in two])
        r0 = restrict([x[2:6] for x in f0])
        r1 = restrict([x[1:5] for x in g1])
        r2 = restrict(g2)
        c0 = coarse_tendency(restrict([o[1:9] for o in old0]))
        c1 = coarse_tendency(restrict(one))
        reach = 8 - 2 * n
        force[n][pl.ds(reach, OWN), 0] = (Q0[0] * r0 + Q0[1] * r1 + Q0[2] * r2) - half_step * c0
        force[n][pl.ds(reach, OWN), 1] = (Q1[0] * r0 + Q1[1] * r1 + Q1[2] * r2) - half_step * c1
        group = []
        for d in range(reach // 2, 0, -1):
            for offset in (d, -d):
                group.append(send(force[n].at[pl.ds(reach, OWN)],
                                  force[n].at[pl.ds(reach - 2 * offset, OWN)], offset))
        force_sends.append(group)
    end_sends = [send(ends.at[2], ends.at[0], 1), send(ends.at[1], ends.at[3], -1)]

    t = coarse[1:21]
    stores = []
    for n in range(SLABS):
        for copy in force_sends[n]:
            copy.wait_recv()
        t = coarse_step(t) + force[n][:, 0]
        reach = 8 - 2 * n
        t = coarse_step(t) + force[n][pl.ds(1, 2 * reach), 1]
        if n == 0:
            for copy in end_sends:
                copy.wait_recv()
        first = 8 - (2 * n + 2)
        moved = prolong(t[first:first + 4] - ends[:, n])
        full = [new[n, k] + moved[k][1:5] for k in range(4)]
        for k, (px, pz) in enumerate(PARITIES):
            stage[1 + n, pz, pl.ds(px, 32, 2)] = full[k].reshape(32, 128)
        x = jnp.concatenate([stage[1 + n, 0], stage[1 + n, 1]], -1)
        obuf[n] = pick(x, join).reshape(4, 16, 256)
        store = pltpu.make_async_copy(obuf.at[n], out_ref.at[n], out_sem.at[n])
        store.start()
        stores.append(store)
    for copy in copies:
        copy.wait_send()
    for store in stores:
        store.wait()


def solution(mesh):
    count = mesh.shape["gy"]

    def body(initial):
        f32 = jnp.float32
        tile = (8, 128)
        sends = 2 * REACH + 2 + 20 + 2
        return pl.pallas_call(
            lambda *refs: kernel(count, *refs),
            out_shape=jax.ShapeDtypeStruct((SLABS,) + initial.shape, f32),
            in_specs=[pl.BlockSpec(memory_space=pl.ANY)],
            out_specs=pl.BlockSpec(memory_space=pl.ANY),
            scratch_shapes=[
                pltpu.VMEM(initial.shape, f32),
                pltpu.VMEM((10, 4) + tile, f32),
                pltpu.VMEM((4 * REACH + OWN,) + tile, f32),
                pltpu.VMEM((18, 2) + tile, f32),
                pltpu.VMEM((14, 2) + tile, f32),
                pltpu.VMEM((10, 2) + tile, f32),
                pltpu.VMEM((6, 2) + tile, f32),
                pltpu.VMEM((4, SLABS) + tile, f32),
                pltpu.VMEM((SLABS, 4, 4) + tile, f32),
                pltpu.VMEM((1 + SLABS, 2, 64, 128), f32),
                pltpu.VMEM((SLABS,) + initial.shape, f32),
                pltpu.SemaphoreType.DMA(()),
                pltpu.SemaphoreType.DMA((SLABS,)),
                pltpu.SemaphoreType.DMA((sends,)),
                pltpu.SemaphoreType.DMA((sends,)),
            ],
            compiler_params=pltpu.CompilerParams(
                collective_id=0, has_side_effects=True, vmem_limit_bytes=32 * 1024 * 1024),
            name="pfasst",
        )(initial)

    return jax.shard_map(body, mesh=mesh, in_specs=(P("gy", "grp", None),),
                         out_specs=P(None, "gy", "grp", None), check_vma=False)
```

time: 275 us -> 23 us (0.08)
  waiting for transfers between devices: 85.6 us -> 0 us
  other arithmetic: 81.4 us -> 0 us
  local copies, waits for them, and re-layouts: 63.1 us -> 1.54 us
  starting transfers between devices: 43.5 us -> 0 us
  Pallas kernels: 0 us -> 21.3 us
    ppermute x42 -> x0, waiting for transfers between devices: 85.6 us -> none  [the longest x21 72.4 us: padded_2(): lax.ppermute(lax.slice_in_dim(block, block.shape[dim] - width, None, axis...]
    reduce_sum x3 -> x0, other arithmetic: 73.1 us -> none  [restrict(): return jnp.mean(blocks, axis=(-5, -3, -1))]
    ppermute x42 -> x0, starting transfers between devices: 43.5 us -> none  [the longest x21 36.7 us: padded_2(): lax.ppermute(lax.slice_in_dim(block, 0, width, axis=dim), axis, backward)]
    pallas_call x0 -> x1, Pallas kernels: none -> 21.3 us  [body(): pl.pallas_call(lambda *refs: kernel(count, *refs), out_shape=jax.ShapeDty...]
    add x4 -> x0, local copies, waits for them, and re-layouts: 19.9 us -> none  [the longest x2 10.5 us: padded_tendency(): coefficient * (beside - 6.0 * center) + (center - center * center * center)]
    slice x101 -> x0, local copies, waits for them, and re-layouts: 19.4 us -> none  [the longest x38 5.95 us: padded_tendency(): beside = beside + jnp.roll(center, 1, -1) + jnp.roll(center, -1, -1)]
    reshape x3 -> x0, local copies, waits for them, and re-layouts: 11.2 us -> none  [the longest x1 6.33 us: restrict(): field.reshape(sizes_now[:-3] + (sizes_now[-3] // 2, 2, sizes_now[-2] // 2...]
    another operation x6 -> x0, local copies, waits for them, and re-layouts: 7.92 us -> none  [alternate(): paired = jnp.stack([even_rows, odd_rows], axis=along)]
  transfers between devices with their start and end apart: 42 -> 0, of which waited for: 33 -> 0; matrix products, arithmetic and copies ran while one was open for 23% -> 0% of each run, Pallas kernels for 0% -> 0%
where the time goes in v1:
time: 23 us; the launch traced here: 22.9 us
  Pallas kernels  21.3 us (93%)
  local copies, waits for them, and re-layouts  1.54 us (7%)
    pallas_call x1, Pallas kernels, body(): pl.pallas_call(lambda *refs: kernel(count, *refs), out_shape=jax.ShapeDty...  21.3 us
    unnamed x3, local copies, waits for them, and re-layouts  1.54 us

profile of v1, /device:TPU:0, one launch (start us, length us, event | category | flops | bytes accessed | tf_op | source)
XLA Modules:
  0.0 22.9 jit_solution(3897481189351822350)
XLA Ops:
  0.0 0.0 copy-start
  0.0 0.8 %copy-done = f32[4,16,256]{2,1,0:T(8,128)S(1)} copy-done((f32[4,16,256]{2,1,0:T(8,128)S(1)}, f32[4,16,256]{2,1,0:T(8,128)}, u32[]{:S(2)}) %copy-start) | copy-done | bytes 65560
  0.8 21.3 %pfasst.1 = f32[4,4,16,256]{3,2,1,0:T(8,128)S(1)} custom-call(f32[4,16,256]{2,1,0:T(8,128)S(1)} %copy-done), custom_call_target="tpu_custom_call" | custom-call | tf_op jit(solution)/shard_map/pfasst/pallas_call | solution.py:214
  22.2 0.7 %copy.3 = f32[4,4,16,256]{3,2,1,0:T(8,128)} copy(f32[4,4,16,256]{3,2,1,0:T(8,128)S(1)} %pfasst.1) | data formatting | bytes 524288
Async XLA Ops:
  0.0 0.8 %copy-start = (f32[4,16,256]{2,1,0:T(8,128)S(1)}, f32[4,16,256]{2,1,0:T(8,128)}, u32[]{:S(2)}) copy-start(f32[4,16,256]{2,1,0:T(8,128)} %refs_0_.1) | copy-start | bytes 196612

commit v2 on v1

--- a/solution.py
+++ b/solution.py
@@ -13,7 +13,7 @@
 Q0 = tuple(slab_time * w for w in left_weights)
 Q1 = tuple(slab_time * w for w in right_weights)
 
-REACH = 5
+REACH = 6
 OWN = 2
 PARITIES = ((0, 0), (0, 1), (1, 0), (1, 1))
 
@@ -84,8 +84,35 @@
     return (dot(high) + dot(middle)) + dot(low)
 
 
-def kernel(count, init_ref, out_ref, raw, fine, coarse, force0, force1, force2, force3, ends, new, stage, obuf,
-           in_sem, out_sem, send_sem, recv_sem):
+def fine_slab(n, reach, old0, old1, old2, force, ends, new):
+    size = 2 * (OWN + 2 * reach)
+    f0 = fine_tendency(old0)
+    f1 = fine_tendency(old1)
+    f2 = fine_tendency(old2)
+    one = [o[1:-1] + ((Q0[0] * x + Q0[1] * y) + Q0[2] * z) for o, x, y, z in zip(old0, f0, f1, f2)]
+    g1 = fine_tendency(one)
+    two = [o[1:-1] + (half_step * g + ((Q1[0] * x[1:-1] + (Q1[1] - half_step) * y[1:-1]) + Q1[2] * z[1:-1]))
+           for o, g, x, y, z in zip(one, g1, f0, f1, f2)]
+    g2 = fine_tendency(two)
+    at = 2 * reach + 1
+    for k in range(4):
+        new[n, k] = two[k][at:at + 4]
+    if reach:
+        ends[n] = restrict([t[at - 2:at + 6] for t in two])
+    else:
+        ends[n, pl.ds(1, OWN)] = restrict([t[1:-1] for t in two])
+    r0 = restrict([x[2:-2] for x in f0])
+    r1 = restrict([x[1:-1] for x in g1])
+    r2 = restrict(g2)
+    c0 = coarse_tendency(restrict([o[1:-1] for o in old0]))
+    c1 = coarse_tendency(restrict(one))
+    where = pl.ds(0 if reach else 8, OWN + 2 * reach)
+    force[where, 0] = (Q0[0] * r0 + Q0[1] * r1 + Q0[2] * r2) - half_step * c0
+    force[where, 1] = (Q1[0] * r0 + Q1[1] * r1 + Q1[2] * r2) - half_step * c1
+
+
+def kernel(count, init_ref, out_ref, raw, fine, coarse, force0, force1, force2, force3, ends, new, stage,
+           in_sem, send_sem, recv_sem):
     me = lax.axis_index("gy")
     force = (force0, force1, force2, force3)
 
@@ -124,84 +151,55 @@
         fine[pl.ds(3, 4), k] = own[k]
 
     pl.semaphore_wait(barrier, 2 * REACH)
-    first_sends = []
-    for d in range(REACH, 0, -1):
+    def send_rows(d):
+        return [send(coarse.at[pl.ds(2 * REACH, OWN)],
+                     coarse.at[pl.ds(2 * REACH - 2 * offset, OWN)], offset) for offset in (d, -d)]
+
+    near = send_rows(1)
+    near += [send(fine.at[pl.ds(4, 3)], fine.at[pl.ds(0, 3)], 1),
+             send(fine.at[pl.ds(3, 3)], fine.at[pl.ds(7, 3)], -1)]
+    near += send_rows(2)
+    far = []
+    for d in range(REACH, 2, -1):
+        far += send_rows(d)
+
+    for copy in near:
+        copy.wait_recv()
+    s = coarse[pl.ds(2 * REACH - 4, OWN + 8)]
+    node1 = coarse_step(s)
+    node2 = coarse_step(node1)
+    fine_slab(0, 0, [fine[:, k] for k in range(4)], prolong(node1[1:-1]), prolong(node2), force0, ends, new)
+    exchange = []
+    for d in range(4, 0, -1):
         for offset in (d, -d):
-            first_sends.append(send(coarse.at[pl.ds(2 * REACH, OWN)],
-                                    coarse.at[pl.ds(2 * REACH - 2 * offset, OWN)], offset))
-    fine_sends = [send(fine.at[pl.ds(4, 3)], fine.at[pl.ds(0, 3)], 1),
-                  send(fine.at[pl.ds(3, 3)], fine.at[pl.ds(7, 3)], -1)]
-
-    for copy in first_sends:
+            exchange.append(send(force0.at[pl.ds(8, OWN)], force0.at[pl.ds(8 - 2 * offset, OWN)], offset))
+    exchange += [send(ends.at[0, 2], ends.at[0, 0], 1), send(ends.at[0, 1], ends.at[0, 3], -1)]
+
+    for copy in far:
         copy.wait_recv()
-    s = coarse[...]
-    nodes = [s[8:14]]
-    for k in range(1, 9):
-        s = coarse_step(s)
-        nodes.append(s[8 - k:14 - k])
-
-    for copy in fine_sends:
+    nodes = [coarse[...]]
+    for k in range(2 * SLABS):
+        nodes.append(coarse_step(nodes[-1]))
+    for n in range(1, SLABS):
+        fine_slab(n, 8 - 2 * n, prolong(nodes[2 * n][2:-2]), prolong(nodes[2 * n + 1][1:-1]),
+                  prolong(nodes[2 * n + 2]), force[n], ends, new)
+
+    t = coarse[2 * REACH - 9:2 * REACH + OWN + 9]
+    for copy in exchange:
         copy.wait_recv()
-    force_sends = []
     for n in range(SLABS):
-        if n == 0:
-            old0 = [fine[:, k] for k in range(4)]
-        else:
-            old0 = prolong(nodes[2 * n])
-        old1 = prolong(nodes[2 * n + 1])
-        old2 = prolong(nodes[2 * n + 2])
-        f0 = fine_tendency(old0)
-        f1 = fine_tendency(old1)
-        f2 = fine_tendency(old2)
-        one = [o[1:-1] + ((Q0[0] * x + Q0[1] * y) + Q0[2] * z) for o, x, y, z in zip(old0, f0, f1, f2)]
-        g1 = fine_tendency(one)
-        two = [o[1:-1] + (half_step * g + ((Q1[0] * x[1:-1] + (Q1[1] - half_step) * y[1:-1]) + Q1[2] * z[1:-1]))
-               for o, g, x, y, z in zip(one, g1, f0, f1, f2)]
-        g2 = fine_tendency(two)
-        for k in range(4):
-            new[n, k] = two[k][1:5]
-        ends[pl.ds(1, 2), n] = restrict([t[1:5] for t in two])
-        r0 = restrict([x[2:6] for x in f0])
-        r1 = restrict([x[1:5] for x in g1])
-        r2 = restrict(g2)
-        c0 = coarse_tendency(restrict([o[1:9] for o in old0]))
-        c1 = coarse_tendency(restrict(one))
         reach = 8 - 2 * n
-        force[n][pl.ds(reach, OWN), 0] = (Q0[0] * r0 + Q0[1] * r1 + Q0[2] * r2) - half_step * c0
-        force[n][pl.ds(reach, OWN), 1] = (Q1[0] * r0 + Q1[1] * r1 + Q1[2] * r2) - half_step * c1
-        group = []
-        for d in range(reach // 2, 0, -1):
-            for offset in (d, -d):
-                group.append(send(force[n].at[pl.ds(reach, OWN)],
-                                  force[n].at[pl.ds(reach - 2 * offset, OWN)], offset))
-        force_sends.append(group)
-    end_sends = [send(ends.at[2], ends.at[0], 1), send(ends.at[1], ends.at[3], -1)]
-
-    t = coarse[1:21]
-    stores = []
-    for n in range(SLABS):
-        for copy in force_sends[n]:
-            copy.wait_recv()
         t = coarse_step(t) + force[n][:, 0]
-        reach = 8 - 2 * n
         t = coarse_step(t) + force[n][pl.ds(1, 2 * reach), 1]
-        if n == 0:
-            for copy in end_sends:
-                copy.wait_recv()
-        first = 8 - (2 * n + 2)
-        moved = prolong(t[first:first + 4] - ends[:, n])
+        first = reach - 2
+        moved = prolong(t[first:first + 4] - ends[n])
         full = [new[n, k] + moved[k][1:5] for k in range(4)]
         for k, (px, pz) in enumerate(PARITIES):
             stage[1 + n, pz, pl.ds(px, 32, 2)] = full[k].reshape(32, 128)
         x = jnp.concatenate([stage[1 + n, 0], stage[1 + n, 1]], -1)
-        obuf[n] = pick(x, join).reshape(4, 16, 256)
-        store = pltpu.make_async_copy(obuf.at[n], out_ref.at[n], out_sem.at[n])
-        store.start()
-        stores.append(store)
+        out_ref[n] = pick(x, join).reshape(4, 16, 256)
     for copy in copies:
         copy.wait_send()
-    for store in stores:
-        store.wait()
 
 
 def solution(mesh):
@@ -210,12 +208,12 @@
     def body(initial):
         f32 = jnp.float32
         tile = (8, 128)
-        sends = 2 * REACH + 2 + 20 + 2
+        sends = 2 * REACH + 2 + 8 + 2
         return pl.pallas_call(
             lambda *refs: kernel(count, *refs),
             out_shape=jax.ShapeDtypeStruct((SLABS,) + initial.shape, f32),
-            in_specs=[pl.BlockSpec(memory_space=pl.ANY)],
-            out_specs=pl.BlockSpec(memory_space=pl.ANY),
+            in_specs=[pl.BlockSpec(memory_space=pltpu.HBM)],
+            out_specs=pl.BlockSpec(memory_space=pltpu.VMEM),
             scratch_shapes=[
                 pltpu.VMEM(initial.shape, f32),
                 pltpu.VMEM((10, 4) + tile, f32),
@@ -224,12 +222,10 @@
                 pltpu.VMEM((14, 2) + tile, f32),
                 pltpu.VMEM((10, 2) + tile, f32),
                 pltpu.VMEM((6, 2) + tile, f32),
-                pltpu.VMEM((4, SLABS) + tile, f32),
+                pltpu.VMEM((SLABS, 4) + tile, f32),
                 pltpu.VMEM((SLABS, 4, 4) + tile, f32),
                 pltpu.VMEM((1 + SLABS, 2, 64, 128), f32),
-                pltpu.VMEM((SLABS,) + initial.shape, f32),
                 pltpu.SemaphoreType.DMA(()),
-                pltpu.SemaphoreType.DMA((SLABS,)),
                 pltpu.SemaphoreType.DMA((sends,)),
                 pltpu.SemaphoreType.DMA((sends,)),
             ],

time: 23 us -> 19.3 us (0.84)
  Pallas kernels: 21.3 us -> 17.6 us
    pallas_call x1, Pallas kernels: 21.3 us -> 17.6 us  [body(): pl.pallas_call(lambda *refs: kernel(count, *refs), out_shape=jax.ShapeDty...]
where the time goes in v2:
time: 19.3 us; the launch traced here: 19.2 us
  Pallas kernels  17.6 us (91%)
  local copies, waits for them, and re-layouts  1.54 us (8%)
    pallas_call x1, Pallas kernels, body(): pl.pallas_call(lambda *refs: kernel(count, *refs), out_shape=jax.ShapeDty...  17.6 us
    unnamed x3, local copies, waits for them, and re-layouts  1.54 us

profile of v2, /device:TPU:0, one launch (start us, length us, event | category | flops | bytes accessed | tf_op | source)
XLA Modules:
  0.0 19.2 jit_solution(9429027629327148440)
XLA Ops:
  0.0 0.0 copy-start
  0.0 0.8 %copy-done = f32[4,16,256]{2,1,0:T(8,128)S(1)} copy-done((f32[4,16,256]{2,1,0:T(8,128)S(1)}, f32[4,16,256]{2,1,0:T(8,128)}, u32[]{:S(2)}) %copy-start) | copy-done | bytes 65560
  0.8 17.6 %pfasst.1 = f32[4,4,16,256]{3,2,1,0:T(8,128)S(1)} custom-call(f32[4,16,256]{2,1,0:T(8,128)S(1)} %copy-done), custom_call_target="tpu_custom_call" | custom-call | tf_op jit(solution)/shard_map/pfasst/pallas_call | solution.py:212
  18.5 0.7 %copy.3 = f32[4,4,16,256]{3,2,1,0:T(8,128)} copy(f32[4,4,16,256]{3,2,1,0:T(8,128)S(1)} %pfasst.1) | data formatting | bytes 524288
Async XLA Ops:
  0.0 0.8 %copy-start = (f32[4,16,256]{2,1,0:T(8,128)S(1)}, f32[4,16,256]{2,1,0:T(8,128)}, u32[]{:S(2)}) copy-start(f32[4,16,256]{2,1,0:T(8,128)} %refs_0_.1) | copy-start | bytes 196612

commit v3 on v2

--- a/solution.py
+++ b/solution.py
@@ -84,7 +84,7 @@
     return (dot(high) + dot(middle)) + dot(low)
 
 
-def fine_slab(n, reach, old0, old1, old2, force, ends, new):
+def fine_slab(n, reach, old0, old1, old2, ends, new):
     size = 2 * (OWN + 2 * reach)
     f0 = fine_tendency(old0)
     f1 = fine_tendency(old1)
@@ -106,21 +106,24 @@
     r2 = restrict(g2)
     c0 = coarse_tendency(restrict([o[1:-1] for o in old0]))
     c1 = coarse_tendency(restrict(one))
-    where = pl.ds(0 if reach else 8, OWN + 2 * reach)
-    force[where, 0] = (Q0[0] * r0 + Q0[1] * r1 + Q0[2] * r2) - half_step * c0
-    force[where, 1] = (Q1[0] * r0 + Q1[1] * r1 + Q1[2] * r2) - half_step * c1
-
-
-def kernel(count, init_ref, out_ref, raw, fine, coarse, force0, force1, force2, force3, ends, new, stage,
-           in_sem, send_sem, recv_sem):
+    return ((Q0[0] * r0 + Q0[1] * r1 + Q0[2] * r2) - half_step * c0,
+            (Q1[0] * r0 + Q1[1] * r1 + Q1[2] * r2) - half_step * c1)
+
+
+def table(axis):
+    wide = lax.broadcasted_iota(jnp.int32, (256, 256), axis)
+    split = lax.broadcasted_iota(jnp.int32, (256, 256), 1 - axis)
+    return (wide == ((split & 127) << 1) + (split >> 7)).astype(jnp.float32).astype(jnp.bfloat16)
+
+
+def kernel(count, init_ref, out_ref, fine, coarse, force0, force1, force2, force3, ends, new, stage,
+           send_sem, recv_sem):
     me = lax.axis_index("gy")
     force = (force0, force1, force2, force3)
 
     def device(offset):
         return {"gy": lax.rem(me + (offset + count), count)}
 
-    fetch = pltpu.make_async_copy(init_ref, raw, in_sem)
-    fetch.start()
     barrier = pltpu.get_barrier_semaphore()
     for d in range(1, REACH + 1):
         for offset in (d, -d):
@@ -136,13 +139,7 @@
         copies.append(copy)
         return copy
 
-    a = lax.broadcasted_iota(jnp.int32, (256, 256), 0)
-    b = lax.broadcasted_iota(jnp.int32, (256, 256), 1)
-    part = (a == 2 * lax.rem(b, 128) + lax.div(b, 128)).astype(jnp.float32).astype(jnp.bfloat16)
-    join = (b == 2 * lax.rem(a, 128) + lax.div(a, 128)).astype(jnp.float32).astype(jnp.bfloat16)
-
-    fetch.wait()
-    y = pick(raw[...].reshape(64, 256), part)
+    y = pick(init_ref[...].reshape(64, 256), table(0))
     stage[0, 0] = y[:, :128]
     stage[0, 1] = y[:, 128:]
     own = [stage[0, pz, pl.ds(px, 32, 2)].reshape(4, 8, 128) for px, pz in PARITIES]
@@ -160,19 +157,24 @@
              send(fine.at[pl.ds(3, 3)], fine.at[pl.ds(7, 3)], -1)]
     near += send_rows(2)
     far = []
-    for d in range(REACH, 2, -1):
+    for d in range(3, REACH + 1):
         far += send_rows(d)
 
+    join = table(1)
     for copy in near:
         copy.wait_recv()
     s = coarse[pl.ds(2 * REACH - 4, OWN + 8)]
     node1 = coarse_step(s)
     node2 = coarse_step(node1)
-    fine_slab(0, 0, [fine[:, k] for k in range(4)], prolong(node1[1:-1]), prolong(node2), force0, ends, new)
+    start, middle = fine_slab(0, 0, [fine[:, k] for k in range(4)], prolong(node1[1:-1]), prolong(node2), ends, new)
+    force0[4, 0] = middle[0]
+    force0[4, 1:3] = start
+    force0[4, 3] = middle[1]
     exchange = []
-    for d in range(4, 0, -1):
+    for d in range(1, 5):
         for offset in (d, -d):
-            exchange.append(send(force0.at[pl.ds(8, OWN)], force0.at[pl.ds(8 - 2 * offset, OWN)], offset))
+            part = pl.ds(0, 4) if d < 4 else pl.ds(1 if offset > 0 else 0, 3)
+            exchange.append(send(force0.at[4, part], force0.at[4 - offset, part], offset))
     exchange += [send(ends.at[0, 2], ends.at[0, 0], 1), send(ends.at[0, 1], ends.at[0, 3], -1)]
 
     for copy in far:
@@ -181,16 +183,24 @@
     for k in range(2 * SLABS):
         nodes.append(coarse_step(nodes[-1]))
     for n in range(1, SLABS):
-        fine_slab(n, 8 - 2 * n, prolong(nodes[2 * n][2:-2]), prolong(nodes[2 * n + 1][1:-1]),
-                  prolong(nodes[2 * n + 2]), force[n], ends, new)
+        start, middle = fine_slab(n, 8 - 2 * n, prolong(nodes[2 * n][2:-2]), prolong(nodes[2 * n + 1][1:-1]),
+                                  prolong(nodes[2 * n + 2]), ends, new)
+        force[n][:, 0] = start
+        force[n][:, 1] = middle
 
     t = coarse[2 * REACH - 9:2 * REACH + OWN + 9]
+    step = coarse_step(t)
     for copy in exchange:
         copy.wait_recv()
     for n in range(SLABS):
         reach = 8 - 2 * n
-        t = coarse_step(t) + force[n][:, 0]
-        t = coarse_step(t) + force[n][pl.ds(1, 2 * reach), 1]
+        if n == 0:
+            start = force0[:, 1:3].reshape(18, 8, 128)
+            middle = jnp.stack([force0[0:8, 3], force0[1:9, 0]], 1).reshape(16, 8, 128)
+        else:
+            start, middle = force[n][:, 0], force[n][pl.ds(1, 2 * reach), 1]
+        t = (step if n == 0 else coarse_step(t)) + start
+        t = coarse_step(t) + middle
         first = reach - 2
         moved = prolong(t[first:first + 4] - ends[n])
         full = [new[n, k] + moved[k][1:5] for k in range(4)]
@@ -212,20 +222,18 @@
         return pl.pallas_call(
             lambda *refs: kernel(count, *refs),
             out_shape=jax.ShapeDtypeStruct((SLABS,) + initial.shape, f32),
-            in_specs=[pl.BlockSpec(memory_space=pltpu.HBM)],
+            in_specs=[pl.BlockSpec(memory_space=pltpu.VMEM)],
             out_specs=pl.BlockSpec(memory_space=pltpu.VMEM),
             scratch_shapes=[
-                pltpu.VMEM(initial.shape, f32),
                 pltpu.VMEM((10, 4) + tile, f32),
                 pltpu.VMEM((4 * REACH + OWN,) + tile, f32),
-                pltpu.VMEM((18, 2) + tile, f32),
+                pltpu.VMEM((9, 4) + tile, f32),
                 pltpu.VMEM((14, 2) + tile, f32),
                 pltpu.VMEM((10, 2) + tile, f32),
                 pltpu.VMEM((6, 2) + tile, f32),
                 pltpu.VMEM((SLABS, 4) + tile, f32),
                 pltpu.VMEM((SLABS, 4, 4) + tile, f32),
                 pltpu.VMEM((1 + SLABS, 2, 64, 128), f32),
-                pltpu.SemaphoreType.DMA(()),
                 pltpu.SemaphoreType.DMA((sends,)),
                 pltpu.SemaphoreType.DMA((sends,)),
             ],

time: 19.3 us -> 18.6 us (0.964)
  Pallas kernels: 17.6 us -> 16.9 us
    pallas_call x1, Pallas kernels: 17.6 us -> 16.9 us  [body(): pl.pallas_call(lambda *refs: kernel(count, *refs), out_shape=jax.ShapeDty...]
where the time goes in v3:
time: 18.6 us; the launch traced here: 18.4 us
  Pallas kernels  16.9 us (91%)
  local copies, waits for them, and re-layouts  1.54 us (8%)
    pallas_call x1, Pallas kernels, body(): pl.pallas_call(lambda *refs: kernel(count, *refs), out_shape=jax.ShapeDty...  16.9 us
    unnamed x3, local copies, waits for them, and re-layouts  1.54 us

profile of v3, /device:TPU:0, one launch (start us, length us, event | category | flops | bytes accessed | tf_op | source)
XLA Modules:
  0.0 18.4 jit_solution(15050505113608641999)
XLA Ops:
  0.0 0.0 copy-start
  0.0 0.8 %copy-done = f32[4,16,256]{2,1,0:T(8,128)S(1)} copy-done((f32[4,16,256]{2,1,0:T(8,128)S(1)}, f32[4,16,256]{2,1,0:T(8,128)}, u32[]{:S(2)}) %copy-start) | copy-done | bytes 65560
  0.8 16.9 %pfasst.1 = f32[4,4,16,256]{3,2,1,0:T(8,128)S(1)} custom-call(f32[4,16,256]{2,1,0:T(8,128)S(1)} %copy-done), custom_call_target="tpu_custom_call" | custom-call | tf_op jit(solution)/shard_map/pfasst/pallas_call | solution.py:222
  17.7 0.7 %copy.3 = f32[4,4,16,256]{3,2,1,0:T(8,128)} copy(f32[4,4,16,256]{3,2,1,0:T(8,128)S(1)} %pfasst.1) | data formatting | bytes 524288
Async XLA Ops:
  0.0 0.8 %copy-start = (f32[4,16,256]{2,1,0:T(8,128)S(1)}, f32[4,16,256]{2,1,0:T(8,128)}, u32[]{:S(2)}) copy-start(f32[4,16,256]{2,1,0:T(8,128)} %refs_0_.1) | copy-start | bytes 196612

commit v4 on v3

--- a/solution.py
+++ b/solution.py
@@ -125,7 +125,7 @@
         return {"gy": lax.rem(me + (offset + count), count)}
 
     barrier = pltpu.get_barrier_semaphore()
-    for d in range(1, REACH + 1):
+    for d in range(REACH, 0, -1):
         for offset in (d, -d):
             pl.semaphore_signal(barrier, inc=1, device_id=device(offset))
 

time: 18.6 us -> 18.6 us (level)
  no operation moved by 1% of the time
where the time goes in v4:
time: 18.6 us; the launch traced here: 18.4 us
  Pallas kernels  16.9 us (91%)
  local copies, waits for them, and re-layouts  1.54 us (8%)
    pallas_call x1, Pallas kernels, body(): pl.pallas_call(lambda *refs: kernel(count, *refs), out_shape=jax.ShapeDty...  16.9 us
    unnamed x3, local copies, waits for them, and re-layouts  1.54 us

profile of v4, /device:TPU:0, one launch (start us, length us, event | category | flops | bytes accessed | tf_op | source)
XLA Modules:
  0.0 18.4 jit_solution(15690161911895648719)
XLA Ops:
  0.0 0.0 copy-start
  0.0 0.8 %copy-done = f32[4,16,256]{2,1,0:T(8,128)S(1)} copy-done((f32[4,16,256]{2,1,0:T(8,128)S(1)}, f32[4,16,256]{2,1,0:T(8,128)}, u32[]{:S(2)}) %copy-start) | copy-done | bytes 65560
  0.8 16.9 %pfasst.1 = f32[4,4,16,256]{3,2,1,0:T(8,128)S(1)} custom-call(f32[4,16,256]{2,1,0:T(8,128)S(1)} %copy-done), custom_call_target="tpu_custom_call" | custom-call | tf_op jit(solution)/shard_map/pfasst/pallas_call | solution.py:222
  17.7 0.7 %copy.3 = f32[4,4,16,256]{3,2,1,0:T(8,128)} copy(f32[4,4,16,256]{3,2,1,0:T(8,128)S(1)} %pfasst.1) | data formatting | bytes 524288
Async XLA Ops:
  0.0 0.8 %copy-start = (f32[4,16,256]{2,1,0:T(8,128)S(1)}, f32[4,16,256]{2,1,0:T(8,128)}, u32[]{:S(2)}) copy-start(f32[4,16,256]{2,1,0:T(8,128)} %refs_0_.1) | copy-start | bytes 196612
